TPU v7x, 32 devices: a whole 2x2x4 slice. The times are simulated.
32 devices in a mesh: dom: 4 (over z), blk: 8 (over y, x, core).
Axes of the slice: x: 2, y: 2, z: 4, core: 2. Of those that a mesh axis runs over, the one named last changes fastest.
Arguments:
- features_domain: bfloat16 [24576, 1152], P(('dom', 'blk')), may hold values from -6 to 6
- arrival: int32 [24576], P(('dom', 'blk')), may hold values from 0 to 767, as said below
- positions: float32 [24576, 3], P(('dom', 'blk')), may hold values from 0 to 768, as said below
- species: int32 [24576], P(('dom', 'blk')), may hold values from 0 to 88
- block_count: int32 [384], P(('dom', 'blk')), may hold values from 16 to 64, as said below
- pair_block: int32 [384, 3], P(('dom', 'blk')), may hold values from -1 to 383, as said below
- radial_weights: float32 [8, 7, 128], replicated, may hold values from -0.75 to 0.75
- species_weights: float32 [89, 3, 128], replicated, may hold values from -1 to 1
- mix_weight: bfloat16 [128, 128], replicated, may hold values from -0.5 to 0.5
- self_weight: bfloat16 [128, 128], replicated, may hold values from -0.5 to 0.5
- readout: float32 [128], replicated, may hold values from -0.5 to 0.5
Outputs:
- atom_energy: float32 [24576], P(('dom', 'blk'))
- forces: float32 [24576, 3], P(('dom', 'blk'))
- new_features: bfloat16 [24576, 128], P(('dom', 'blk'))
Inputs may be any that keep to these rules, and one draw needn't show every extreme that they name: `arrival`: on each device of dom+blk its 768 entries are a permutation of 0 to 767. `pair_block`: entry [b, 0] is b - 1 or -1, entry [b, 1] is b, entry [b, 2] is b + 1 or -1; the lists are symmetric: [b, 2] is b + 1 exactly when [b + 1, 0] is b. The first block has no predecessor and the last no successor. `block_count`: the live atoms of a block are its first slots. `positions`: atoms of blocks that are not paired lie a distance of 1 or more apart.
All inputs are finite; a program needn't handle non-finite values.
Results may differ from a plain program's by a relative error of at most 0.015.
Values may be sent and summed in bfloat16 or wider, within the bound.
No kernel may reach another device: no remote copies, remote signals or barrier semaphores. Data moves between devices by JAX's collectives and lax.ppermute only.
A program may use at most 64 MiB of HBM per device.

v0:
```python
import functools
import math

import jax
import jax.numpy as jnp
import numpy as np
from jax import lax
from jax.experimental import pallas as pl
from jax.experimental.pallas import tpu as pltpu
from jax.sharding import PartitionSpec as P

BLOCK = 64
TILE = 2 * BLOCK
WINDOW = 4 * BLOCK
SUB = BLOCK
HARM = 9
PATHS = 7
ROOT_THREE = math.sqrt(3.0)
AXES = ("dom", "blk")
VMEM_BYTES = 48 * 1024 * 1024
HELD = pltpu.VMEM


def degree(k):
    return 0 if k == 0 else (1 if k < 4 else 2)


def polynomial(square, coefficients):
    total = jnp.full_like(square, coefficients[-1])
    for value in coefficients[-2::-1]:
        total = total * square + value
    return total


SINE = [(-1.0) ** m * math.pi ** (2 * m + 1) / math.factorial(2 * m + 1) for m in range(6)]
COSINE = [(-1.0) ** m * math.pi ** (2 * m) / math.factorial(2 * m) for m in range(7)]


def solid(x, y, z):
    return [
        None,
        x,
        y,
        z,
        ROOT_THREE * x * y,
        ROOT_THREE * y * z,
        z * z - 0.5 * (x * x + y * y),
        ROOT_THREE * z * x,
        (0.5 * ROOT_THREE) * (x * x - y * y),
    ]


def chosen_rows(wanted, rows):
    source = lax.broadcasted_iota(jnp.int32, (wanted.shape[0], rows), 1)
    return (wanted == source).astype(jnp.float32).astype(jnp.bfloat16)


def as_column(row_ref):
    return jnp.transpose(jnp.broadcast_to(row_ref[...], (8, row_ref.shape[1])))[:, 0:1]


def edge_tiles_kernel(arrival_ref, received_ref, first_ref, last_ref):
    rows = received_ref.shape[0]
    wanted = as_column(arrival_ref)
    both = jnp.concatenate([wanted[0:TILE], wanted[rows - TILE :]], axis=0)
    found = jnp.dot(
        chosen_rows(both, rows), received_ref[...], preferred_element_type=jnp.float32
    ).astype(jnp.bfloat16)
    first_ref[...] = found[0:TILE]
    last_ref[...] = found[TILE:]


def pair_factors(base, rows_ref, cols_ref, edge_at, value_at, change_at, orders):
    window = pl.ds(base, WINDOW)
    for sub in range(TILE // SUB):
        half = sub * SUB // BLOCK
        here = pl.ds(pl.multiple_of(base + (BLOCK + sub * SUB), SUB), SUB)
        column = lax.broadcasted_iota(jnp.int32, (SUB, WINDOW), 1)
        row = lax.broadcasted_iota(jnp.int32, (SUB, WINDOW), 0) + (sub * SUB + BLOCK)
        offset = column - half * BLOCK
        low = jnp.where((offset >= 0) & (offset < BLOCK), cols_ref[here, 5:6], 0.0)
        high = jnp.where(
            (offset >= 2 * BLOCK) & (offset < 3 * BLOCK), cols_ref[here, 6:7], low
        )
        same = (offset >= BLOCK) & (offset < 2 * BLOCK) & (row != column)
        keep = jnp.where(same, 1.0, high)
        x, y, z = [rows_ref[a : a + 1, window] - cols_ref[here, a : a + 1] for a in range(3)]
        spread = x * x + y * y + z * z
        room = jnp.maximum(1.0 - spread, 0.0)
        squared = room * room * keep
        envelope = squared * room
        slope = -3.0 * squared
        shifted = jnp.minimum(spread, 1.0) - 0.5
        shifted_sq = shifted * shifted
        cosine = -shifted * polynomial(shifted_sq, SINE)
        sine = polynomial(shifted_sq, COSINE)
        twice = 2.0 * cosine
        cos_prev, cos_now = jnp.ones_like(cosine), cosine
        sin_prev, sin_now = jnp.zeros_like(sine), sine
        harm = solid(x, y, z)
        for n in range(orders):
            rows = slice(n * SUB, (n + 1) * SUB)
            if n == 0:
                value, change = envelope, slope
            else:
                value = envelope * cos_now
                change = slope * cos_now - (n * math.pi) * (envelope * sin_now)
            value_at[sub, rows, :] = value.astype(jnp.bfloat16)
            change_at[sub, rows, :] = change.astype(jnp.bfloat16)
            for k in range(HARM):
                edge = value if k == 0 else value * harm[k]
                edge_at[sub, k, rows, :] = edge.astype(jnp.bfloat16)
            if n >= 1:
                cos_prev, cos_now = cos_now, twice * cos_now - cos_prev
                sin_prev, sin_now = sin_now, twice * sin_now - sin_prev


def pairs_kernel(rows_ref, edge_ref, value_ref, change_ref, cols_ref, orders):
    tile = pl.program_id(0)

    @pl.when(tile == 0)
    def _():
        cols_ref[...] = jnp.transpose(rows_ref[...])

    base = pl.multiple_of(tile * TILE, TILE)
    pair_factors(
        base, rows_ref, cols_ref, edge_ref.at[0], value_ref.at[0], change_ref.at[0], orders
    )


def spread_weights(radial_ref, narrow_ref, orders):
    for path in range(PATHS):
        for n in range(orders):
            row = radial_ref[n * PATHS + path : n * PATHS + path + 1, :]
            narrow_ref[path, n * SUB : (n + 1) * SUB, :] = jnp.broadcast_to(
                row, (SUB, row.shape[1])
            ).astype(jnp.bfloat16)


def fetch(sources, held):
    edge_hbm, value_hbm, change_hbm = sources
    edge_ref, value_ref, change_ref, edge_sem, factor_sem = held
    count, subs = edge_ref.shape[:2]

    def edges(at, sub):
        return pltpu.make_async_copy(
            edge_hbm.at[at, sub], edge_ref.at[at, sub], edge_sem.at[at, sub]
        )

    def factors(at):
        return (
            pltpu.make_async_copy(value_hbm.at[at], value_ref.at[at], factor_sem.at[at, 0]),
            pltpu.make_async_copy(change_hbm.at[at], change_ref.at[at], factor_sem.at[at, 1]),
        )

    for at in range(count):
        for sub in range(subs):
            edges(at, sub).start()
        for copy in factors(at):
            copy.start()
    return edges, factors


def one_tile(at, base, refs, gain_of, copies, results, orders):
    feat_ref, turned_ref, rows_ref, cols_ref, edge_ref, value_ref, change_ref = refs[:7]
    radial_ref, narrow_ref, mix_ref, self_ref, readout_ref = refs[7:12]
    message_ref, grad_ref = refs[12:]
    channels = mix_ref.shape[0]
    window = pl.ds(base, WINDOW)
    centre = pl.ds(pl.multiple_of(base + BLOCK, BLOCK), TILE)
    subs = range(TILE // SUB)

    def weight(n, path):
        return radial_ref[n * PATHS + path : n * PATHS + path + 1, :]

    def piece(k):
        return feat_ref[window, k * channels : (k + 1) * channels]

    def path_sum(product, first, path):
        total = None
        for n in range(orders):
            part = product[n * SUB : (n + 1) * SUB, first : first + channels] * weight(n, path)
            total = part if total is None else total + part
        return total

    for sub in subs:
        rows = slice(sub * SUB, (sub + 1) * SUB)
        if copies is not None:
            copies[0](at, sub).wait()
        found = {}
        for k in range(0, HARM, 2):
            last = min(k + 2, HARM)
            pairs = jnp.dot(
                edge_ref[at, sub, 0],
                feat_ref[window, k * channels : last * channels],
                preferred_element_type=jnp.float32,
            )
            for which in range(k, last):
                path = 0 if which == 0 else 2 + degree(which)
                found[which] = path_sum(pairs, (which - k) * channels, path)
        for k in range(1, HARM):
            both = jnp.concatenate([piece(k), piece(0)], axis=1)
            pairs = jnp.dot(edge_ref[at, sub, k], both, preferred_element_type=jnp.float32)
            found[0] = found[0] + path_sum(pairs, 0, 4 + degree(k))
            message_ref[k, rows, :] = found[k] + path_sum(pairs, channels, degree(k))
        message_ref[0, rows, :] = found[0]

    gain = gain_of(centre)
    zero = message_ref[0]
    first = sum(message_ref[k] * message_ref[k] for k in range(1, 4))
    second = sum(message_ref[k] * message_ref[k] for k in range(4, HARM))
    basis = zero + gain[0] * (zero * zero) + gain[1] * first + gain[2] * second
    live = cols_ref[centre, 3:4]
    mixed = jnp.dot(
        basis.astype(jnp.bfloat16), mix_ref[...], preferred_element_type=jnp.float32
    ) + jnp.dot(feat_ref[centre, 0:channels], self_ref[...], preferred_element_type=jnp.float32)
    gate = 1.0 / (1.0 + jnp.exp(-mixed))
    silu = mixed * gate
    readout = readout_ref[...]
    fresh = (live * mixed).astype(jnp.bfloat16)
    energy = jnp.sum(jnp.transpose(live * (readout * silu)), axis=0, keepdims=True)
    mixed_grad = live * readout * (gate * (1.0 + mixed - silu))
    basis_grad = lax.dot_general(
        mixed_grad.astype(jnp.bfloat16),
        mix_ref[...],
        (((1,), (1,)), ((), ())),
        preferred_element_type=jnp.float32,
    )
    grad_ref[0] = (basis_grad * (1.0 + 2.0 * gain[0] * zero)).astype(jnp.bfloat16)
    for k in range(1, HARM):
        grad_ref[k] = (basis_grad * (2.0 * gain[degree(k)]) * message_ref[k]).astype(jnp.bfloat16)

    def backward(sub):
        rows = slice(sub * SUB, (sub + 1) * SUB)
        here = pl.ds(pl.multiple_of(base + (BLOCK + sub * SUB), SUB), SUB)
        grads = [jnp.concatenate([grad_ref[k, rows, :]] * orders, axis=0) for k in range(HARM)]
        x, y, z = [rows_ref[a : a + 1, window] - cols_ref[here, a : a + 1] for a in range(3)]
        harm = solid(x, y, z)
        root_x, root_y, root_z = ROOT_THREE * x, ROOT_THREE * y, ROOT_THREE * z
        slopes = {
            1: {0: None},
            2: {1: None},
            3: {2: None},
            4: {0: root_y, 1: root_x},
            5: {1: root_z, 2: root_y},
            6: {0: -x, 1: -y, 2: 2.0 * z},
            7: {0: root_z, 2: root_x},
            8: {0: root_x, 1: -root_y},
        }

        def over_orders(cross, factor_ref):
            parts = [
                cross[n * SUB : (n + 1) * SUB].astype(jnp.bfloat16)
                * factor_ref[at, sub, n * SUB : (n + 1) * SUB, :]
                for n in range(orders)
            ]
            while len(parts) > 1:
                parts = [parts[m] + parts[m + 1] for m in range(0, len(parts), 2)]
            return parts[0].astype(jnp.float32)

        left = jnp.concatenate(
            [grads[k] * narrow_ref[0 if k == 0 else 2 + degree(k)] for k in range(HARM)], axis=1
        )
        cross = jnp.dot(left, turned_ref[:, window], preferred_element_type=jnp.float32)
        radial_total = over_orders(cross, change_ref)
        pull = [None, None, None]
        for k in range(1, HARM):
            left = jnp.concatenate(
                [grads[0] * narrow_ref[4 + degree(k)], grads[k] * narrow_ref[degree(k)]], axis=1
            )
            both = jnp.concatenate(
                [
                    turned_ref[k * channels : (k + 1) * channels, window],
                    turned_ref[0:channels, window],
                ],
                axis=0,
            )
            cross = jnp.dot(left, both, preferred_element_type=jnp.float32)
            along = over_orders(cross, value_ref)
            radial_total = radial_total + over_orders(cross, change_ref) * harm[k]
            for axis, factor in slopes[k].items():
                term = along if factor is None else along * factor
                pull[axis] = term if pull[axis] is None else pull[axis] + term
        radial_total = 2.0 * radial_total
        return [pull[axis] + delta * radial_total for axis, delta in enumerate((x, y, z))]

    if copies is not None:
        for copy in copies[1](at):
            copy.wait()
    onto_window = [None, None, None]
    columns_out = [[], [], []]
    for sub in subs:
        for axis, total in enumerate(backward(sub)):
            summed = jnp.sum(total, axis=0, keepdims=True)
            onto_window[axis] = summed if sub == 0 else onto_window[axis] + summed
            columns_out[axis].append(jnp.sum(total, axis=1, keepdims=True))
    lane = lax.broadcasted_iota(jnp.int32, (TILE, 8), 1)
    row = lax.broadcasted_iota(jnp.int32, (8, WINDOW), 0)
    packed = jnp.zeros((TILE, 8), jnp.float32)
    pulled = jnp.zeros((8, WINDOW), jnp.float32)
    for axis in range(3):
        packed = jnp.where(lane == axis, jnp.concatenate(columns_out[axis], axis=0), packed)
        pulled = jnp.where(row == axis, onto_window[axis], pulled)
    turned = jnp.transpose(packed)
    side = jnp.zeros((8, BLOCK), jnp.float32)
    results(fresh, energy, jnp.concatenate([side, turned, side], axis=1) - pulled)


def inner_kernel(
    arrival_ref,
    received_ref,
    first_ref,
    last_ref,
    rows_ref,
    edge_hbm,
    value_hbm,
    change_hbm,
    gains_ref,
    radial_ref,
    mix_ref,
    self_ref,
    readout_ref,
    feat_ref,
    new_ref,
    energy_ref,
    force_ref,
    turned_ref,
    cols_ref,
    narrow_ref,
    message_ref,
    grad_ref,
    edge_ref,
    value_ref,
    change_ref,
    edge_sem,
    factor_sem,
    orders,
):
    held = (edge_ref, value_ref, change_ref, edge_sem, factor_sem)
    copies = fetch((edge_hbm, value_hbm, change_hbm), held)
    rows = received_ref.shape[0]
    channels = mix_ref.shape[0]
    wanted = as_column(arrival_ref)
    cols_ref[...] = jnp.transpose(rows_ref[...])
    spread_weights(radial_ref, narrow_ref, orders)
    force_ref[...] = jnp.zeros_like(force_ref)
    feat_ref[0:TILE, :] = first_ref[...]
    turned_ref[:, 0:TILE] = jnp.transpose(first_ref[...])
    for part in range(1, rows // TILE - 1):
        here = slice(part * TILE, (part + 1) * TILE)
        found = jnp.dot(
            chosen_rows(wanted[here], rows),
            received_ref[...],
            preferred_element_type=jnp.float32,
        ).astype(jnp.bfloat16)
        feat_ref[here, :] = found
        turned_ref[:, here] = jnp.transpose(found)
    feat_ref[rows - TILE :, :] = last_ref[...]
    turned_ref[:, rows - TILE :] = jnp.transpose(last_ref[...])
    refs = (feat_ref, turned_ref, rows_ref, cols_ref, edge_ref, value_ref, change_ref)
    refs += (radial_ref, narrow_ref, mix_ref, self_ref, readout_ref, message_ref, grad_ref)

    def gain_of(centre):
        return [gains_ref[centre, l * channels : (l + 1) * channels] for l in range(3)]

    def body(at, carry):
        base = pl.multiple_of(at * TILE, TILE)

        def results(fresh, energy, force):
            new_ref[at] = fresh
            energy_ref[at] = energy
            force_ref[:, pl.ds(base, WINDOW)] += force

        one_tile(at, base, refs, gain_of, copies, results, orders)
        return carry

    lax.fori_loop(0, edge_hbm.shape[0], body, 0)


def outer_kernel(
    low_ref,
    high_ref,
    feat_ref,
    low_rows_ref,
    rows_ref,
    high_rows_ref,
    table_ref,
    radial_ref,
    mix_ref,
    self_ref,
    readout_ref,
    inner_new_ref,
    inner_energy_ref,
    inner_force_ref,
    new_ref,
    energy_ref,
    force_ref,
    near_ref,
    turned_ref,
    near_rows_ref,
    cols_ref,
    narrow_ref,
    message_ref,
    grad_ref,
    edge_ref,
    value_ref,
    change_ref,
    total_ref,
    orders,
):
    rows = feat_ref.shape[0]
    channels = mix_ref.shape[0]
    near_rows_ref[:, 0:TILE] = low_rows_ref[...]
    near_rows_ref[:, TILE : 2 * TILE] = rows_ref[:, 0:TILE]
    near_rows_ref[:, 2 * TILE : 3 * TILE] = rows_ref[:, rows - TILE :]
    near_rows_ref[:, 3 * TILE :] = high_rows_ref[...]
    cols_ref[...] = jnp.transpose(near_rows_ref[...])
    spread_weights(radial_ref, narrow_ref, orders)
    near_ref[0:TILE, :] = low_ref[...]
    near_ref[TILE : 2 * TILE, :] = feat_ref[0:TILE, :]
    near_ref[2 * TILE : 3 * TILE, :] = feat_ref[rows - TILE :, :]
    near_ref[3 * TILE :, :] = high_ref[...]
    for part in range(4):
        here = slice(part * TILE, (part + 1) * TILE)
        turned_ref[:, here] = jnp.transpose(near_ref[here, :])
    refs = (near_ref, turned_ref, near_rows_ref, cols_ref, edge_ref, value_ref, change_ref)
    refs += (radial_ref, narrow_ref, mix_ref, self_ref, readout_ref, message_ref, grad_ref)

    def gain_of(centre):
        kinds = lax.broadcasted_iota(jnp.int32, (TILE, table_ref.shape[0]), 1)
        picked = (cols_ref[centre, 4:5].astype(jnp.int32) == kinds).astype(jnp.float32)
        rows_of = jnp.dot(
            picked,
            table_ref[...],
            precision=lax.Precision.HIGHEST,
            preferred_element_type=jnp.float32,
        )
        return [rows_of[:, l * channels : (l + 1) * channels] for l in range(3)]

    def body(at, carry):
        base = pl.multiple_of(at * WINDOW, WINDOW)

        def results(fresh, energy, force):
            total_ref[at] = force

            if at == 0:
                new_ref[0:BLOCK, :] = fresh[BLOCK:, :]
                energy_ref[0:BLOCK] = energy[0, BLOCK:]

            if at == 1:
                new_ref[rows - BLOCK :, :] = fresh[0:BLOCK, :]
                energy_ref[rows - BLOCK :] = energy[0, 0:BLOCK]

        pair_factors(
            base, near_rows_ref, cols_ref, edge_ref.at[at], value_ref.at[at], change_ref.at[at], orders
        )
        one_tile(at, base, refs, gain_of, None, results, orders)
        return carry

    for at in range(2):
        body(at, 0)
    inner = inner_new_ref.shape[0]
    for at in range(inner):
        here = slice(BLOCK + at * TILE, BLOCK + (at + 1) * TILE)
        new_ref[here, :] = inner_new_ref[at]
        energy_ref[here] = inner_energy_ref[at, 0]
    force_ref[...] = inner_force_ref[0:3, :]
    force_ref[:, 0:TILE] += total_ref[0, 0:3, TILE:]
    force_ref[:, rows - TILE :] += total_ref[1, 0:3, 0:TILE]


def call(kernel, name, out_shape, scratch, flops, *operands, distant=()):
    whole = pl.BlockSpec(memory_space=pltpu.VMEM)
    hbm = pl.BlockSpec(memory_space=pl.ANY)
    return pl.pallas_call(
        kernel,
        out_shape=out_shape,
        in_specs=[hbm if at in distant else whole for at in range(len(operands))],
        out_specs=jax.tree.map(lambda _: whole, out_shape),
        scratch_shapes=scratch,
        compiler_params=pltpu.CompilerParams(vmem_limit_bytes=VMEM_BYTES),
        cost_estimate=pl.CostEstimate(flops=flops, bytes_accessed=4 * 2**20, transcendentals=0),
        name=name,
    )(*operands)


def from_sides(block_low, block_high):
    count = lax.axis_size(AXES)
    forward = [(i, i + 1) for i in range(count - 1)]
    backward = [(target, source) for source, target in forward]
    low = lax.ppermute(block_high, AXES, forward)
    high = lax.ppermute(block_low, AXES, backward)
    return low, high


def per_device(
    features_domain,
    arrival,
    positions,
    species,
    block_count,
    pair_block,
    radial_weights,
    species_weights,
    mix_weight,
    self_weight,
    readout,
):
    devices = lax.axis_size(AXES)
    atom_rows, feature_cols = features_domain.shape
    piece_rows = atom_rows // devices
    parcels = features_domain.reshape(devices, piece_rows, feature_cols)
    received = lax.all_to_all(parcels, AXES, split_axis=0, concat_axis=0, tiled=True)
    received = received.reshape(atom_rows, feature_cols)
    blocks = block_count.shape[0]
    bf16, f32 = jnp.bfloat16, jnp.float32
    shape = jax.ShapeDtypeStruct

    def per_slot(values):
        return jnp.broadcast_to(values[:, None], (blocks, BLOCK)).reshape(1, atom_rows)

    slot = jnp.arange(BLOCK, dtype=jnp.int32)
    live = (slot[None, :] < block_count[:, None]).reshape(1, atom_rows)
    arrival_live = jnp.where(live, arrival.reshape(1, atom_rows), -1)
    listed = (pair_block >= 0).astype(f32)
    rows = jnp.concatenate(
        [
            positions.T,
            live.astype(f32),
            species.astype(f32).reshape(1, atom_rows),
            per_slot(listed[:, 0]),
            per_slot(listed[:, 2]),
            jnp.zeros((1, atom_rows), f32),
        ],
        axis=0,
    )
    low_rows, high_rows = from_sides(rows[:, :TILE], rows[:, atom_rows - TILE :])
    species_total = species_weights.shape[0]
    one_hot = (species[:, None] == jnp.arange(species_total, dtype=jnp.int32)[None, :]).astype(f32)
    table = species_weights.reshape(species_total, -1)
    gains = jnp.dot(one_hot, table, precision=lax.Precision.HIGHEST)
    orders, _, channels = radial_weights.shape
    inner = atom_rows // TILE - 1
    subs = TILE // SUB
    stack = orders * SUB
    edges, values, changes = pl.pallas_call(
        functools.partial(pairs_kernel, orders=orders),
        grid=(inner,),
        out_shape=(
            pltpu.HBM((inner, subs, HARM, stack, WINDOW), bf16),
            pltpu.HBM((inner, subs, stack, WINDOW), bf16),
            pltpu.HBM((inner, subs, stack, WINDOW), bf16),
        ),
        in_specs=[pl.BlockSpec((8, atom_rows), lambda t: (0, 0))],
        out_specs=(
            pl.BlockSpec((1, subs, HARM, stack, WINDOW), lambda t: (t, 0, 0, 0, 0)),
            pl.BlockSpec((1, subs, stack, WINDOW), lambda t: (t, 0, 0, 0)),
            pl.BlockSpec((1, subs, stack, WINDOW), lambda t: (t, 0, 0, 0)),
        ),
        scratch_shapes=[pltpu.VMEM((atom_rows, 8), f32)],
        compiler_params=pltpu.CompilerParams(vmem_limit_bytes=VMEM_BYTES),
        cost_estimate=pl.CostEstimate(flops=10**10, bytes_accessed=40 * 2**20, transcendentals=0),
        name="pairs",
    )(rows)
    first, last = call(
        edge_tiles_kernel,
        "edge_tiles",
        (shape((TILE, feature_cols), bf16), shape((TILE, feature_cols), bf16)),
        [],
        4 * TILE * atom_rows * feature_cols,
        arrival_live,
        received,
    )
    low, high = from_sides(first, last)
    radial = radial_weights.reshape(-1, channels)
    common = (radial, mix_weight, self_weight, readout.reshape(1, -1))
    tile_flops = 4 * orders * TILE * WINDOW * channels * 25
    held = functools.partial(pltpu.with_memory_space_constraint, memory_space=pltpu.VMEM)
    distant = functools.partial(pltpu.with_memory_space_constraint, memory_space=pltpu.HBM)

    def scratch(count):
        return [
            pltpu.VMEM((PATHS, orders * SUB, channels), bf16),
            pltpu.VMEM((HARM, TILE, channels), f32),
            pltpu.VMEM((HARM, TILE, channels), bf16),
            pltpu.VMEM((count, subs, HARM, stack, WINDOW), bf16),
            pltpu.VMEM((count, subs, stack, WINDOW), bf16),
            pltpu.VMEM((count, subs, stack, WINDOW), bf16),
        ]

    feat, inner_new, inner_energy, inner_force = call(
        functools.partial(inner_kernel, orders=orders),
        "inner",
        (
            HELD((atom_rows, feature_cols), bf16),
            HELD((inner, TILE, channels), bf16),
            HELD((inner, 1, TILE), f32),
            HELD((8, atom_rows), f32),
        ),
        [pltpu.VMEM((feature_cols, atom_rows), bf16), pltpu.VMEM((atom_rows, 8), f32)]
        + scratch(inner)
        + [pltpu.SemaphoreType.DMA((inner, subs)), pltpu.SemaphoreType.DMA((inner, 2))],
        inner * tile_flops,
        arrival_live,
        received,
        first,
        last,
        rows,
        distant(edges),
        distant(values),
        distant(changes),
        gains,
        *common,
        distant=(5, 6, 7),
    )
    new_rows, energies, forces = call(
        functools.partial(outer_kernel, orders=orders),
        "outer",
        (
            shape((atom_rows, channels), bf16),
            shape((atom_rows,), f32),
            shape((3, atom_rows), f32),
        ),
        [
            pltpu.VMEM((4 * TILE, feature_cols), bf16),
            pltpu.VMEM((feature_cols, 4 * TILE), bf16),
            pltpu.VMEM((8, 4 * TILE), f32),
            pltpu.VMEM((4 * TILE, 8), f32),
        ]
        + scratch(2)
        + [pltpu.VMEM((2, 8, WINDOW), f32)],
        2 * tile_flops,
        low,
        high,
        held(feat),
        low_rows,
        rows,
        high_rows,
        table,
        *common,
        held(inner_new),
        held(inner_energy),
        held(inner_force),
    )
    return (energies, forces.T, new_rows)


def solution(mesh):
    placed = (
        P(("dom", "blk"), None),
        P(("dom", "blk")),
        P(("dom", "blk"), None),
        P(("dom", "blk")),
        P(("dom", "blk")),
        P(("dom", "blk"), None),
        P(),
        P(),
        P(),
        P(),
        P(),
    )
    return jax.shard_map(
        per_device,
        mesh=mesh,
        in_specs=placed,
        out_specs=(P(("dom", "blk")), P(("dom", "blk"), None), P(("dom", "blk"), None)),
        check_vma=False,
    )
```

profile of v0, /device:TPU:4, one launch (start us, length us, event | category | flops | bytes accessed | tf_op | source)
XLA Modules:
  0.0 96.2 jit_solution(4361497397800176803)
XLA Ops:
  0.6 0.0 copy-start.8
  0.6 0.0 copy-start.9
  0.7 0.0 copy-start.5
  0.7 0.0 copy-start.6
  0.7 0.0 copy-start.7
  0.7 6.1 %all-to-all-start = ((bf16[32,24,1152]{2,1,0:T(8,128)(2,1)}), bf16[32,24,1152]{2,1,0:T(8,128)(2,1)S(1)}, u32[]{:S(2)}, u32[]{:S(2)}) async-start(bf16[32,24,1152]{2,1,0:T(8,128)(2,1)} %bitcast.19), calls=%async_computation | async-start | bytes 3538944 | tf_op jit(solution)/shard_map/all_to_all | solution.py:513
  6.8 0.1 broadcast_in_dim.27
  6.9 0.1 reshape.69
  7.0 0.1 broadcast_in_dim.29
  7.1 0.1 reshape.70
  7.2 0.1 fusion.2
  7.2 0.1 reshape.74
  7.4 2.1 %collective-permute-start.2 = (f32[8,128]{1,0:T(8,128)S(1)}, f32[8,128]{1,0:T(8,128)S(1)}, u32[]{:S(2)}, u32[]{:S(2)}) collective-permute-start(f32[8,128]{1,0:T(8,128)S(1)} %get-tuple-element.28), channel_id=1, source_target_pairs={{0,1},{1,2},{2,3},{3,4},{4,5},{5,6},{6,7},{7,8},{8,9},{9,10},{10,1... | collective-permute-start | bytes 12296 | tf_op jit(solution)/shard_map/ppermute | solution.py:491
  9.5 4.4 %collective-permute-start.3 = (f32[8,128]{1,0:T(8,128)S(1)}, f32[8,128]{1,0:T(8,128)S(1)}, u32[]{:S(2)}, u32[]{:S(2)}) collective-permute-start(f32[8,128]{1,0:T(8,128)S(1)} %get-tuple-element.27), channel_id=1, source_target_pairs={{1,0},{2,1},{3,2},{4,3},{5,4},{6,5},{7,6},{8,7},{9,8},{10,9},{11,1... | collective-permute-start | bytes 12296 | tf_op jit(solution)/shard_map/ppermute | solution.py:492
  13.9 0.1 lt.29
  14.0 0.1 copy.16
  14.2 0.0 copy-done.4
  14.2 0.7 fusion.gains_ref
  14.9 11.5 %pairs.1 = (bf16[5,2,9,512,256]{4,3,2,1,0:T(8,128)(2,1)}, bf16[5,2,512,256]{3,2,1,0:T(8,128)(2,1)}, bf16[5,2,512,256]{3,2,1,0:T(8,128)(2,1)}) custom-call(f32[8,768]{1,0:T(8,128)S(1)} %concatenate.3.rows_ref), custom_call_target="tpu_custom_call" | custom-call | flops 10000000000 | bytes 41943040 | tf_op jit(solution)/shard_map/pairs/pallas_call | solution.py:546
  26.4 21.8 %all-to-all-done = bf16[32,24,1152]{2,1,0:T(8,128)(2,1)S(1)} async-done(((bf16[32,24,1152]{2,1,0:T(8,128)(2,1)}), bf16[32,24,1152]{2,1,0:T(8,128)(2,1)S(1)}, u32[]{:S(2)}, u32[]{:S(2)}) %all-to-all-start) | async-done | bytes 1769504 | tf_op jit(solution)/shard_map/all_to_all | solution.py:513
  48.2 0.9 edge_tiles.1
  49.1 1.9 %collective-permute-start = (bf16[128,1152]{1,0:T(8,128)(2,1)S(1)}, bf16[128,1152]{1,0:T(8,128)(2,1)S(1)}, u32[]{:S(2)}, u32[]{:S(2)}) collective-permute-start(bf16[128,1152]{1,0:T(8,128)(2,1)S(1)} %get-tuple-element.15.last_ref), channel_id=1, source_target_pairs={{0,1},{1,2},{2,3},{3,4},{4,5},{5,6},{6,7},{7,8},{8,9},{9,10},{10,1... | collective-permute-start | bytes 884744 | tf_op jit(solution)/shard_map/ppermute | solution.py:491
  51.0 4.5 %collective-permute-start.1 = (bf16[128,1152]{1,0:T(8,128)(2,1)S(1)}, bf16[128,1152]{1,0:T(8,128)(2,1)S(1)}, u32[]{:S(2)}, u32[]{:S(2)}) collective-permute-start(bf16[128,1152]{1,0:T(8,128)(2,1)S(1)} %get-tuple-element.16.first_ref), channel_id=1, source_target_pairs={{1,0},{2,1},{3,2},{4,3},{5,4},{6,5},{7,6},{8,7},{9,8},{10,9},{11,1... | collective-permute-start | bytes 884744 | tf_op jit(solution)/shard_map/ppermute | solution.py:492
  55.5 0.0 copy-done
  55.6 0.0 copy-done.1
  55.6 0.0 copy-done.2
  55.6 28.8 %inner.1 = (bf16[768,1152]{1,0:T(8,128)(2,1)S(1)}, bf16[5,128,128]{2,1,0:T(8,128)(2,1)S(1)}, f32[5,1,128]{2,1,0:T(1,128)S(1)}, f32[8,768]{1,0:T(8,128)S(1)}) custom-call(s32[1,768]{1,0:T(1,128)S(1)} %select_n.7.arrival_ref, bf16[768,1152]{1,0:T(8,128)(2,1)S(1)} %bitcast.14, bf16[128,1152]{1,0:T(8,128)(2,1)S(1)} %get-tuple-element.16.first_ref, ...), custom_call_target="tpu_custom_call" | custom-call | flops 16777216000 | bytes 4194304 | tf_op jit(solution)/shard_map/inner/pallas_call | solution.py:475
  84.4 0.0 collective-permute-done.2.low_rows_ref
  84.4 0.0 collective-permute-done.3.high_rows_ref
  84.4 0.0 collective-permute-done.low_ref
  84.4 0.0 collective-permute-done.1.high_ref
  84.4 11.8 %outer.1 = (bf16[768,128]{1,0:T(8,128)(2,1)}, f32[768]{0:T(1024)}, f32[3,768]{1,0:T(4,128)}) custom-call(bf16[128,1152]{1,0:T(8,128)(2,1)S(1)} %collective-permute-done.low_ref, bf16[128,1152]{1,0:T(8,128)(2,1)S(1)} %collective-permute-done.1.high_ref, bf16[768,1152]{1,0:T(8,128)(2,1)S(1)} %get-tuple-element.20.feat_ref, ...), custom_call_target="tpu_custom_call" | custom-call | flops 6710886400 | bytes 4194304 | tf_op jit(solution)/shard_map/outer/pallas_call | solution.py:475
  (24 shorter events, 0.2 us)
Async XLA Ops:
  0.6 6.2 %copy-start.8 = (s32[12,3]{0,1:T(4,128)S(1)}, s32[12,3]{0,1:T(4,128)}, u32[]{:S(2)}) copy-start(s32[12,3]{0,1:T(4,128)} %param.16) | copy-start | bytes 436
  0.6 6.5 %copy-start.9 = (s32[12]{0:T(128)S(1)}, s32[12]{0:T(128)}, u32[]{:S(2)}) copy-start(s32[12]{0:T(128)} %param.15) | copy-start | bytes 148
  0.7 6.7 %copy-start.5 = (s32[768]{0:T(1024)S(1)}, s32[768]{0:T(1024)}, u32[]{:S(2)}) copy-start(s32[768]{0:T(1024)} %param.14) | copy-start | bytes 9220
  0.7 6.7 %copy-start.6 = (f32[768,3]{0,1:T(4,128)S(1)}, f32[768,3]{0,1:T(4,128)}, u32[]{:S(2)}) copy-start(f32[768,3]{0,1:T(4,128)} %param.13) | copy-start | bytes 27652
  0.7 13.3 %copy-start.7 = (s32[768]{0:T(1024)S(1)}, s32[768]{0:T(1024)}, u32[]{:S(2)}) copy-start(s32[768]{0:T(1024)} %param.12) | copy-start | bytes 9220
  0.7 13.3 %copy-start.3 = (f32[89,3,128]{2,0,1:T(8,128)S(1)}, f32[89,3,128]{2,0,1:T(8,128)}, u32[]{:S(2)}) copy-start(f32[89,3,128]{2,0,1:T(8,128)} %param.18) | copy-start | bytes 410116
  0.7 13.5 %copy-start.4 = (f32[8,7,128]{2,0,1:T(8,128)S(1)}, f32[8,7,128]{2,0,1:T(8,128)}, u32[]{:S(2)}) copy-start(f32[8,7,128]{2,0,1:T(8,128)} %param.17) | copy-start | bytes 86020
  0.7 47.5 %all-to-all-start = ((bf16[32,24,1152]{2,1,0:T(8,128)(2,1)}), bf16[32,24,1152]{2,1,0:T(8,128)(2,1)S(1)}, u32[]{:S(2)}, u32[]{:S(2)}) async-start(bf16[32,24,1152]{2,1,0:T(8,128)(2,1)} %bitcast.19), calls=%async_computation | async-start | bytes 3538944 | tf_op jit(solution)/shard_map/all_to_all | solution.py:513
  7.4 77.0 %collective-permute-start.2 = (f32[8,128]{1,0:T(8,128)S(1)}, f32[8,128]{1,0:T(8,128)S(1)}, u32[]{:S(2)}, u32[]{:S(2)}) collective-permute-start(f32[8,128]{1,0:T(8,128)S(1)} %get-tuple-element.28), channel_id=1, source_target_pairs={{0,1},{1,2},{2,3},{3,4},{4,5},{5,6},{6,7},{7,8},{8,9},{9,10},{10,1... | collective-permute-start | bytes 12296 | tf_op jit(solution)/shard_map/ppermute | solution.py:491
  9.5 74.9 %collective-permute-start.3 = (f32[8,128]{1,0:T(8,128)S(1)}, f32[8,128]{1,0:T(8,128)S(1)}, u32[]{:S(2)}, u32[]{:S(2)}) collective-permute-start(f32[8,128]{1,0:T(8,128)S(1)} %get-tuple-element.27), channel_id=1, source_target_pairs={{1,0},{2,1},{3,2},{4,3},{5,4},{6,5},{7,6},{8,7},{9,8},{10,9},{11,1... | collective-permute-start | bytes 12296 | tf_op jit(solution)/shard_map/ppermute | solution.py:492
  26.4 29.1 %copy-start = (bf16[128,128]{1,0:T(8,128)(2,1)S(1)}, bf16[128,128]{1,0:T(8,128)(2,1)}, u32[]{:S(2)}) copy-start(bf16[128,128]{1,0:T(8,128)(2,1)} %mix_ref.3) | copy-start | bytes 98308
  26.4 29.1 %copy-start.1 = (bf16[128,128]{1,0:T(8,128)(2,1)S(1)}, bf16[128,128]{1,0:T(8,128)(2,1)}, u32[]{:S(2)}) copy-start(bf16[128,128]{1,0:T(8,128)(2,1)} %self_ref.3) | copy-start | bytes 98308
  26.4 29.1 %copy-start.2 = (f32[128]{0:T(128)S(1)}, f32[128]{0:T(128)}, u32[]{:S(2)}) copy-start(f32[128]{0:T(128)} %param.21) | copy-start | bytes 1540
  49.1 35.3 %collective-permute-start = (bf16[128,1152]{1,0:T(8,128)(2,1)S(1)}, bf16[128,1152]{1,0:T(8,128)(2,1)S(1)}, u32[]{:S(2)}, u32[]{:S(2)}) collective-permute-start(bf16[128,1152]{1,0:T(8,128)(2,1)S(1)} %get-tuple-element.15.last_ref), channel_id=1, source_target_pairs={{0,1},{1,2},{2,3},{3,4},{4,5},{5,6},{6,7},{7,8},{8,9},{9,10},{10,1... | collective-permute-start | bytes 884744 | tf_op jit(solution)/shard_map/ppermute | solution.py:491
  51.0 33.4 %collective-permute-start.1 = (bf16[128,1152]{1,0:T(8,128)(2,1)S(1)}, bf16[128,1152]{1,0:T(8,128)(2,1)S(1)}, u32[]{:S(2)}, u32[]{:S(2)}) collective-permute-start(bf16[128,1152]{1,0:T(8,128)(2,1)S(1)} %get-tuple-element.16.first_ref), channel_id=1, source_target_pairs={{1,0},{2,1},{3,2},{4,3},{5,4},{6,5},{7,6},{8,7},{9,8},{10,9},{11,1... | collective-permute-start | bytes 884744 | tf_op jit(solution)/shard_map/ppermute | solution.py:492
where the time goes:
time: 96.4 us; the launch traced here: 96.2 us
  Pallas kernels  52.9 us (55%)
  waiting for transfers between devices  21.8 us (23%)
  starting transfers between devices  19 us (20%)
    pallas_call x3, Pallas kernels, call(): pl.pallas_call(kernel, out_shape=out_shape, in_specs=[hbm if at in distan...  41.4 us
    all_to_all x1, waiting for transfers between devices, per_device(): lax.all_to_all(parcels, AXES, split_axis=0, concat_axis=0, tiled=True)  21.8 us
    pallas_call x1, Pallas kernels, per_device(): pl.pallas_call(functools.partial(pairs_kernel, orders=orders), grid=(inne...  11.5 us
    ppermute x2, starting transfers between devices, from_sides(): high = lax.ppermute(block_low, AXES, backward)  8.95 us
    all_to_all x1, starting transfers between devices, per_device(): lax.all_to_all(parcels, AXES, split_axis=0, concat_axis=0, tiled=True)  6.1 us
    ppermute x2, starting transfers between devices, from_sides(): low = lax.ppermute(block_high, AXES, forward)  3.98 us
  transfers between devices with their start and end apart: 5, of which 1 were waited for; matrix products, arithmetic and copies ran while one was open for 2% of the time, Pallas kernels for 43%

commit v1 on v0

--- a/solution.py
+++ b/solution.py
@@ -17,7 +17,7 @@
 PATHS = 7
 ROOT_THREE = math.sqrt(3.0)
 AXES = ("dom", "blk")
-VMEM_BYTES = 48 * 1024 * 1024
+VMEM_BYTES = 40 * 1024 * 1024
 HELD = pltpu.VMEM
 
 
@@ -50,22 +50,12 @@
     ]
 
 
-def chosen_rows(wanted, rows):
-    source = lax.broadcasted_iota(jnp.int32, (wanted.shape[0], rows), 1)
-    return (wanted == source).astype(jnp.float32).astype(jnp.bfloat16)
-
-
-def as_column(row_ref):
-    return jnp.transpose(jnp.broadcast_to(row_ref[...], (8, row_ref.shape[1])))[:, 0:1]
-
-
-def edge_tiles_kernel(arrival_ref, received_ref, first_ref, last_ref):
+def edge_tiles_kernel(chosen_ref, received_ref, first_ref, last_ref):
     rows = received_ref.shape[0]
-    wanted = as_column(arrival_ref)
-    both = jnp.concatenate([wanted[0:TILE], wanted[rows - TILE :]], axis=0)
-    found = jnp.dot(
-        chosen_rows(both, rows), received_ref[...], preferred_element_type=jnp.float32
-    ).astype(jnp.bfloat16)
+    both = jnp.concatenate([chosen_ref[0:TILE, :], chosen_ref[rows - TILE :, :]], axis=0)
+    found = jnp.dot(both, received_ref[...], preferred_element_type=jnp.float32).astype(
+        jnp.bfloat16
+    )
     first_ref[...] = found[0:TILE]
     last_ref[...] = found[TILE:]
 
@@ -161,7 +151,7 @@
     return edges, factors
 
 
-def one_tile(at, base, refs, gain_of, copies, results, orders):
+def one_tile(at, base, refs, gain_of, copies, results, orders, reach=(None, None)):
     feat_ref, turned_ref, rows_ref, cols_ref, edge_ref, value_ref, change_ref = refs[:7]
     radial_ref, narrow_ref, mix_ref, self_ref, readout_ref = refs[7:12]
     message_ref, grad_ref = refs[12:]
@@ -231,10 +221,12 @@
         grad_ref[k] = (basis_grad * (2.0 * gain[degree(k)]) * message_ref[k]).astype(jnp.bfloat16)
 
     def backward(sub):
+        lanes = slice(0, WINDOW) if reach[sub] is None else reach[sub]
+        seen = pl.ds(pl.multiple_of(base + lanes.start, TILE), lanes.stop - lanes.start)
         rows = slice(sub * SUB, (sub + 1) * SUB)
         here = pl.ds(pl.multiple_of(base + (BLOCK + sub * SUB), SUB), SUB)
         grads = [jnp.concatenate([grad_ref[k, rows, :]] * orders, axis=0) for k in range(HARM)]
-        x, y, z = [rows_ref[a : a + 1, window] - cols_ref[here, a : a + 1] for a in range(3)]
+        x, y, z = [rows_ref[a : a + 1, seen] - cols_ref[here, a : a + 1] for a in range(3)]
         harm = solid(x, y, z)
         root_x, root_y, root_z = ROOT_THREE * x, ROOT_THREE * y, ROOT_THREE * z
         slopes = {
@@ -251,7 +243,7 @@
         def over_orders(cross, factor_ref):
             parts = [
                 cross[n * SUB : (n + 1) * SUB].astype(jnp.bfloat16)
-                * factor_ref[at, sub, n * SUB : (n + 1) * SUB, :]
+                * factor_ref[at, sub, n * SUB : (n + 1) * SUB, lanes]
                 for n in range(orders)
             ]
             while len(parts) > 1:
@@ -261,7 +253,7 @@
         left = jnp.concatenate(
             [grads[k] * narrow_ref[0 if k == 0 else 2 + degree(k)] for k in range(HARM)], axis=1
         )
-        cross = jnp.dot(left, turned_ref[:, window], preferred_element_type=jnp.float32)
+        cross = jnp.dot(left, turned_ref[:, seen], preferred_element_type=jnp.float32)
         radial_total = over_orders(cross, change_ref)
         pull = [None, None, None]
         for k in range(1, HARM):
@@ -270,8 +262,8 @@
             )
             both = jnp.concatenate(
                 [
-                    turned_ref[k * channels : (k + 1) * channels, window],
-                    turned_ref[0:channels, window],
+                    turned_ref[k * channels : (k + 1) * channels, seen],
+                    turned_ref[0:channels, seen],
                 ],
                 axis=0,
             )
@@ -292,6 +284,10 @@
     for sub in subs:
         for axis, total in enumerate(backward(sub)):
             summed = jnp.sum(total, axis=0, keepdims=True)
+            if reach[sub] is not None:
+                rest = jnp.zeros((1, WINDOW - summed.shape[1]), jnp.float32)
+                order = [rest, summed] if reach[sub].start > 0 else [summed, rest]
+                summed = jnp.concatenate(order, axis=1)
             onto_window[axis] = summed if sub == 0 else onto_window[axis] + summed
             columns_out[axis].append(jnp.sum(total, axis=1, keepdims=True))
     lane = lax.broadcasted_iota(jnp.int32, (TILE, 8), 1)
@@ -307,7 +303,7 @@
 
 
 def inner_kernel(
-    arrival_ref,
+    chosen_ref,
     received_ref,
     first_ref,
     last_ref,
@@ -340,7 +336,6 @@
     copies = fetch((edge_hbm, value_hbm, change_hbm), held)
     rows = received_ref.shape[0]
     channels = mix_ref.shape[0]
-    wanted = as_column(arrival_ref)
     cols_ref[...] = jnp.transpose(rows_ref[...])
     spread_weights(radial_ref, narrow_ref, orders)
     force_ref[...] = jnp.zeros_like(force_ref)
@@ -349,7 +344,7 @@
     for part in range(1, rows // TILE - 1):
         here = slice(part * TILE, (part + 1) * TILE)
         found = jnp.dot(
-            chosen_rows(wanted[here], rows),
+            chosen_ref[here, :],
             received_ref[...],
             preferred_element_type=jnp.float32,
         ).astype(jnp.bfloat16)
@@ -386,6 +381,7 @@
     high_rows_ref,
     table_ref,
     radial_ref,
+    narrow_ref,
     mix_ref,
     self_ref,
     readout_ref,
@@ -399,7 +395,6 @@
     turned_ref,
     near_rows_ref,
     cols_ref,
-    narrow_ref,
     message_ref,
     grad_ref,
     edge_ref,
@@ -415,7 +410,6 @@
     near_rows_ref[:, 2 * TILE : 3 * TILE] = rows_ref[:, rows - TILE :]
     near_rows_ref[:, 3 * TILE :] = high_rows_ref[...]
     cols_ref[...] = jnp.transpose(near_rows_ref[...])
-    spread_weights(radial_ref, narrow_ref, orders)
     near_ref[0:TILE, :] = low_ref[...]
     near_ref[TILE : 2 * TILE, :] = feat_ref[0:TILE, :]
     near_ref[2 * TILE : 3 * TILE, :] = feat_ref[rows - TILE :, :]
@@ -454,7 +448,8 @@
         pair_factors(
             base, near_rows_ref, cols_ref, edge_ref.at[at], value_ref.at[at], change_ref.at[at], orders
         )
-        one_tile(at, base, refs, gain_of, None, results, orders)
+        reach = (slice(TILE, WINDOW), None) if at == 0 else (None, slice(0, TILE))
+        one_tile(at, base, refs, gain_of, None, results, orders, reach)
         return carry
 
     for at in range(2):
@@ -521,7 +516,8 @@
 
     slot = jnp.arange(BLOCK, dtype=jnp.int32)
     live = (slot[None, :] < block_count[:, None]).reshape(1, atom_rows)
-    arrival_live = jnp.where(live, arrival.reshape(1, atom_rows), -1)
+    arrival_live = jnp.where(live, arrival.reshape(1, atom_rows), -1).reshape(atom_rows, 1)
+    chosen = (arrival_live == jnp.arange(atom_rows, dtype=jnp.int32)[None, :]).astype(bf16)
     listed = (pair_block >= 0).astype(f32)
     rows = jnp.concatenate(
         [
@@ -568,11 +564,12 @@
         (shape((TILE, feature_cols), bf16), shape((TILE, feature_cols), bf16)),
         [],
         4 * TILE * atom_rows * feature_cols,
-        arrival_live,
+        chosen,
         received,
     )
     low, high = from_sides(first, last)
     radial = radial_weights.reshape(-1, channels)
+    narrow = jnp.repeat(radial_weights.transpose(1, 0, 2).astype(bf16), SUB, axis=1)
     common = (radial, mix_weight, self_weight, readout.reshape(1, -1))
     tile_flops = 4 * orders * TILE * WINDOW * channels * 25
     held = functools.partial(pltpu.with_memory_space_constraint, memory_space=pltpu.VMEM)
@@ -580,7 +577,6 @@
 
     def scratch(count):
         return [
-            pltpu.VMEM((PATHS, orders * SUB, channels), bf16),
             pltpu.VMEM((HARM, TILE, channels), f32),
             pltpu.VMEM((HARM, TILE, channels), bf16),
             pltpu.VMEM((count, subs, HARM, stack, WINDOW), bf16),
@@ -597,11 +593,15 @@
             HELD((inner, 1, TILE), f32),
             HELD((8, atom_rows), f32),
         ),
-        [pltpu.VMEM((feature_cols, atom_rows), bf16), pltpu.VMEM((atom_rows, 8), f32)]
+        [
+            pltpu.VMEM((feature_cols, atom_rows), bf16),
+            pltpu.VMEM((atom_rows, 8), f32),
+            pltpu.VMEM((PATHS, orders * SUB, channels), bf16),
+        ]
         + scratch(inner)
         + [pltpu.SemaphoreType.DMA((inner, subs)), pltpu.SemaphoreType.DMA((inner, 2))],
         inner * tile_flops,
-        arrival_live,
+        chosen,
         received,
         first,
         last,
@@ -637,7 +637,9 @@
         rows,
         high_rows,
         table,
-        *common,
+        radial,
+        narrow,
+        *common[1:],
         held(inner_new),
         held(inner_energy),
         held(inner_force),

time: 96.4 us -> 94.9 us (0.984)
  Pallas kernels: 52.9 us -> 51.2 us
  waiting for transfers between devices: 21.8 us -> 20.5 us
  matrix products: 0.68 us -> 1.77 us
    pallas_call x3, Pallas kernels: 41.4 us -> 39.7 us  [call(): pl.pallas_call(kernel, out_shape=out_shape, in_specs=[hbm if at in distan...]
    all_to_all x1, waiting for transfers between devices: 21.8 us -> 20.5 us  [per_device(): lax.all_to_all(parcels, AXES, split_axis=0, concat_axis=0, tiled=True)]
    dot_general x1, matrix products: 0.68 us -> 1.77 us  [per_device(): gains = jnp.dot(one_hot, table, precision=lax.Precision.HIGHEST)]
  transfers between devices with their start and end apart: 5 -> 5, of which waited for: 1 -> 1; matrix products, arithmetic and copies ran while one was open for 2% -> 3% of each run, Pallas kernels for 43% -> 42%
where the time goes in v1:
time: 94.9 us; the launch traced here: 94.6 us
  Pallas kernels  51.2 us (54%)
  waiting for transfers between devices  20.5 us (22%)
  starting transfers between devices  19 us (20%)
  matrix products  1.77 us (2%)
  between operations  0.95 us (1%)
    pallas_call x3, Pallas kernels, call(): pl.pallas_call(kernel, out_shape=out_shape, in_specs=[hbm if at in distan...  39.7 us
    all_to_all x1, waiting for transfers between devices, per_device(): lax.all_to_all(parcels, AXES, split_axis=0, concat_axis=0, tiled=True)  20.5 us
    pallas_call x1, Pallas kernels, per_device(): pl.pallas_call(functools.partial(pairs_kernel, orders=orders), grid=(inne...  11.5 us
    ppermute x2, starting transfers between devices, from_sides(): high = lax.ppermute(block_low, AXES, backward)  8.95 us
    all_to_all x1, starting transfers between devices, per_device(): lax.all_to_all(parcels, AXES, split_axis=0, concat_axis=0, tiled=True)  6.1 us
    ppermute x2, starting transfers between devices, from_sides(): low = lax.ppermute(block_high, AXES, forward)  3.98 us
  transfers between devices with their start and end apart: 5, of which 1 were waited for; matrix products, arithmetic and copies ran while one was open for 3% of the time, Pallas kernels for 42%

profile of v1, /device:TPU:4, one launch (start us, length us, event | category | flops | bytes accessed | tf_op | source)
XLA Modules:
  0.0 94.6 jit_solution(15902804075208139689)
XLA Ops:
  0.6 0.0 copy-start.9
  0.6 0.0 copy-start.10
  0.7 6.1 %all-to-all-start = ((bf16[32,24,1152]{2,1,0:T(8,128)(2,1)}), bf16[32,24,1152]{2,1,0:T(8,128)(2,1)S(1)}, u32[]{:S(2)}, u32[]{:S(2)}) async-start(bf16[32,24,1152]{2,1,0:T(8,128)(2,1)} %bitcast.23), calls=%async_computation | async-start | bytes 3538944 | tf_op jit(solution)/shard_map/all_to_all | solution.py:508
  6.8 0.1 broadcast_in_dim.31
  6.9 0.1 reshape.75
  7.0 0.1 broadcast_in_dim.33
  7.1 0.1 reshape.76
  7.2 0.1 fusion.3
  7.2 0.1 reshape.81
  7.4 2.1 %collective-permute-start.2 = (f32[8,128]{1,0:T(8,128)S(1)}, f32[8,128]{1,0:T(8,128)S(1)}, u32[]{:S(2)}, u32[]{:S(2)}) collective-permute-start(f32[8,128]{1,0:T(8,128)S(1)} %get-tuple-element.28), channel_id=1, source_target_pairs={{0,1},{1,2},{2,3},{3,4},{4,5},{5,6},{6,7},{7,8},{8,9},{9,10},{10,1... | collective-permute-start | bytes 12296 | tf_op jit(solution)/shard_map/ppermute | solution.py:486
  9.5 4.4 %collective-permute-start.3 = (f32[8,128]{1,0:T(8,128)S(1)}, f32[8,128]{1,0:T(8,128)S(1)}, u32[]{:S(2)}, u32[]{:S(2)}) collective-permute-start(f32[8,128]{1,0:T(8,128)S(1)} %get-tuple-element.27), channel_id=1, source_target_pairs={{1,0},{2,1},{3,2},{4,3},{5,4},{6,5},{7,6},{8,7},{9,8},{10,9},{11,1... | collective-permute-start | bytes 12296 | tf_op jit(solution)/shard_map/ppermute | solution.py:487
  13.9 0.1 lt.29
  14.0 0.0 copy-done.4
  14.0 0.1 copy.16
  14.2 0.3 fusion.chosen_ref
  14.5 1.8 %fusion.1.gains_ref = f32[768,384]{1,0:T(8,128)} fusion(f32[89,384]{1,0:T(8,128)S(1)} %bitcast.19, s32[768]{0:T(1024)S(1)} %copy-done.6), kind=kOutput, calls=%fused_computation.3 | convolution fusion | flops 315034368 | bytes 1319424 | tf_op jit(solution)/shard_map/dot_general | solution.py:537
  16.2 11.5 %pairs.1 = (bf16[5,2,9,512,256]{4,3,2,1,0:T(8,128)(2,1)}, bf16[5,2,512,256]{3,2,1,0:T(8,128)(2,1)}, bf16[5,2,512,256]{3,2,1,0:T(8,128)(2,1)}) custom-call(f32[8,768]{1,0:T(8,128)S(1)} %concatenate.3.rows_ref), custom_call_target="tpu_custom_call" | custom-call | flops 10000000000 | bytes 41943040 | tf_op jit(solution)/shard_map/pairs/pallas_call | solution.py:542
  27.7 20.5 %all-to-all-done = bf16[32,24,1152]{2,1,0:T(8,128)(2,1)S(1)} async-done(((bf16[32,24,1152]{2,1,0:T(8,128)(2,1)}), bf16[32,24,1152]{2,1,0:T(8,128)(2,1)S(1)}, u32[]{:S(2)}, u32[]{:S(2)}) %all-to-all-start) | async-done | bytes 1769504 | tf_op jit(solution)/shard_map/all_to_all | solution.py:508
  48.2 0.7 edge_tiles.1
  48.9 1.9 %collective-permute-start = (bf16[128,1152]{1,0:T(8,128)(2,1)S(1)}, bf16[128,1152]{1,0:T(8,128)(2,1)S(1)}, u32[]{:S(2)}, u32[]{:S(2)}) collective-permute-start(bf16[128,1152]{1,0:T(8,128)(2,1)S(1)} %get-tuple-element.15.last_ref), channel_id=1, source_target_pairs={{0,1},{1,2},{2,3},{3,4},{4,5},{5,6},{6,7},{7,8},{8,9},{9,10},{10,1... | collective-permute-start | bytes 884744 | tf_op jit(solution)/shard_map/ppermute | solution.py:486
  50.8 4.5 %collective-permute-start.1 = (bf16[128,1152]{1,0:T(8,128)(2,1)S(1)}, bf16[128,1152]{1,0:T(8,128)(2,1)S(1)}, u32[]{:S(2)}, u32[]{:S(2)}) collective-permute-start(bf16[128,1152]{1,0:T(8,128)(2,1)S(1)} %get-tuple-element.16.first_ref), channel_id=1, source_target_pairs={{1,0},{2,1},{3,2},{4,3},{5,4},{6,5},{7,6},{8,7},{9,8},{10,9},{11,1... | collective-permute-start | bytes 884744 | tf_op jit(solution)/shard_map/ppermute | solution.py:487
  55.4 0.0 copy-done.1
  55.4 0.0 copy-done.2
  55.4 0.0 copy-done.3
  55.4 0.0 copy-done
  55.4 27.6 %inner.1 = (bf16[768,1152]{1,0:T(8,128)(2,1)S(1)}, bf16[5,128,128]{2,1,0:T(8,128)(2,1)S(1)}, f32[5,1,128]{2,1,0:T(1,128)S(1)}, f32[8,768]{1,0:T(8,128)S(1)}) custom-call(bf16[768,768]{1,0:T(8,128)(2,1)S(1)} %fusion.chosen_ref, bf16[768,1152]{1,0:T(8,128)(2,1)S(1)} %bitcast.17, bf16[128,1152]{1,0:T(8,128)(2,1)S(1)} %get-tuple-element.16.first_ref, ...), custom_call_target="tpu_custom_call" | custom-call | flops 16777216000 | bytes 4194304 | tf_op jit(solution)/shard_map/inner/pallas_call | solution.py:470
  83.0 0.0 collective-permute-done.2.low_rows_ref
  83.0 0.0 collective-permute-done.3.high_rows_ref
  83.0 0.0 collective-permute-done.low_ref
  83.1 0.0 collective-permute-done.1.high_ref
  83.1 0.1 broadcast_in_dim.35
  83.2 11.4 %outer.1 = (bf16[768,128]{1,0:T(8,128)(2,1)}, f32[768]{0:T(1024)}, f32[3,768]{1,0:T(4,128)}) custom-call(bf16[128,1152]{1,0:T(8,128)(2,1)S(1)} %collective-permute-done.low_ref, bf16[128,1152]{1,0:T(8,128)(2,1)S(1)} %collective-permute-done.1.high_ref, bf16[768,1152]{1,0:T(8,128)(2,1)S(1)} %get-tuple-element.20.feat_ref, ...), custom_call_target="tpu_custom_call" | custom-call | flops 6710886400 | bytes 4194304 | tf_op jit(solution)/shard_map/outer/pallas_call | solution.py:470
  (28 shorter events, 0.2 us)
Async XLA Ops:
  0.6 6.2 %copy-start.9 = (s32[12,3]{0,1:T(4,128)S(1)}, s32[12,3]{0,1:T(4,128)}, u32[]{:S(2)}) copy-start(s32[12,3]{0,1:T(4,128)} %param.16) | copy-start | bytes 436
  0.6 6.5 %copy-start.10 = (s32[12]{0:T(128)S(1)}, s32[12]{0:T(128)}, u32[]{:S(2)}) copy-start(s32[12]{0:T(128)} %param.15) | copy-start | bytes 148
  0.7 6.7 %copy-start.6 = (s32[768]{0:T(1024)S(1)}, s32[768]{0:T(1024)}, u32[]{:S(2)}) copy-start(s32[768]{0:T(1024)} %param.14) | copy-start | bytes 9220
  0.7 6.7 %copy-start.7 = (f32[768,3]{0,1:T(4,128)S(1)}, f32[768,3]{0,1:T(4,128)}, u32[]{:S(2)}) copy-start(f32[768,3]{0,1:T(4,128)} %param.13) | copy-start | bytes 27652
  0.7 13.3 %copy-start.4 = (f32[89,3,128]{2,0,1:T(8,128)S(1)}, f32[89,3,128]{2,0,1:T(8,128)}, u32[]{:S(2)}) copy-start(f32[89,3,128]{2,0,1:T(8,128)} %param.18) | copy-start | bytes 410116
  0.7 13.4 %copy-start.5 = (f32[8,7,128]{2,0,1:T(8,128)S(1)}, f32[8,7,128]{2,0,1:T(8,128)}, u32[]{:S(2)}) copy-start(f32[8,7,128]{2,0,1:T(8,128)} %param.17) | copy-start | bytes 86020
  0.7 13.5 %copy-start.8 = (s32[768]{0:T(1024)S(1)}, s32[768]{0:T(1024)}, u32[]{:S(2)}) copy-start(s32[768]{0:T(1024)} %param.12) | copy-start | bytes 9220
  0.7 47.5 %all-to-all-start = ((bf16[32,24,1152]{2,1,0:T(8,128)(2,1)}), bf16[32,24,1152]{2,1,0:T(8,128)(2,1)S(1)}, u32[]{:S(2)}, u32[]{:S(2)}) async-start(bf16[32,24,1152]{2,1,0:T(8,128)(2,1)} %bitcast.23), calls=%async_computation | async-start | bytes 3538944 | tf_op jit(solution)/shard_map/all_to_all | solution.py:508
  7.4 75.6 %collective-permute-start.2 = (f32[8,128]{1,0:T(8,128)S(1)}, f32[8,128]{1,0:T(8,128)S(1)}, u32[]{:S(2)}, u32[]{:S(2)}) collective-permute-start(f32[8,128]{1,0:T(8,128)S(1)} %get-tuple-element.28), channel_id=1, source_target_pairs={{0,1},{1,2},{2,3},{3,4},{4,5},{5,6},{6,7},{7,8},{8,9},{9,10},{10,1... | collective-permute-start | bytes 12296 | tf_op jit(solution)/shard_map/ppermute | solution.py:486
  9.5 73.6 %collective-permute-start.3 = (f32[8,128]{1,0:T(8,128)S(1)}, f32[8,128]{1,0:T(8,128)S(1)}, u32[]{:S(2)}, u32[]{:S(2)}) collective-permute-start(f32[8,128]{1,0:T(8,128)S(1)} %get-tuple-element.27), channel_id=1, source_target_pairs={{1,0},{2,1},{3,2},{4,3},{5,4},{6,5},{7,6},{8,7},{9,8},{10,9},{11,1... | collective-permute-start | bytes 12296 | tf_op jit(solution)/shard_map/ppermute | solution.py:487
  27.7 27.7 %copy-start.1 = (bf16[128,128]{1,0:T(8,128)(2,1)S(1)}, bf16[128,128]{1,0:T(8,128)(2,1)}, u32[]{:S(2)}) copy-start(bf16[128,128]{1,0:T(8,128)(2,1)} %mix_ref.3) | copy-start | bytes 98308
  27.7 27.7 %copy-start.2 = (bf16[128,128]{1,0:T(8,128)(2,1)S(1)}, bf16[128,128]{1,0:T(8,128)(2,1)}, u32[]{:S(2)}) copy-start(bf16[128,128]{1,0:T(8,128)(2,1)} %self_ref.3) | copy-start | bytes 98308
  27.7 27.7 %copy-start.3 = (f32[128]{0:T(128)S(1)}, f32[128]{0:T(128)}, u32[]{:S(2)}) copy-start(f32[128]{0:T(128)} %param.21) | copy-start | bytes 1540
  48.2 7.2 %copy-start = (f32[768,384]{1,0:T(8,128)S(1)}, f32[768,384]{1,0:T(8,128)}, u32[]{:S(2)}) copy-start(f32[768,384]{1,0:T(8,128)} %fusion.1.gains_ref) | copy-start | bytes 3538948
  48.9 34.1 %collective-permute-start = (bf16[128,1152]{1,0:T(8,128)(2,1)S(1)}, bf16[128,1152]{1,0:T(8,128)(2,1)S(1)}, u32[]{:S(2)}, u32[]{:S(2)}) collective-permute-start(bf16[128,1152]{1,0:T(8,128)(2,1)S(1)} %get-tuple-element.15.last_ref), channel_id=1, source_target_pairs={{0,1},{1,2},{2,3},{3,4},{4,5},{5,6},{6,7},{7,8},{8,9},{9,10},{10,1... | collective-permute-start | bytes 884744 | tf_op jit(solution)/shard_map/ppermute | solution.py:486
  50.8 32.2 %collective-permute-start.1 = (bf16[128,1152]{1,0:T(8,128)(2,1)S(1)}, bf16[128,1152]{1,0:T(8,128)(2,1)S(1)}, u32[]{:S(2)}, u32[]{:S(2)}) collective-permute-start(bf16[128,1152]{1,0:T(8,128)(2,1)S(1)} %get-tuple-element.16.first_ref), channel_id=1, source_target_pairs={{1,0},{2,1},{3,2},{4,3},{5,4},{6,5},{7,6},{8,7},{9,8},{10,9},{11,1... | collective-permute-start | bytes 884744 | tf_op jit(solution)/shard_map/ppermute | solution.py:487

commit v2 on v1

--- a/solution.py
+++ b/solution.py
@@ -17,7 +17,7 @@
 PATHS = 7
 ROOT_THREE = math.sqrt(3.0)
 AXES = ("dom", "blk")
-VMEM_BYTES = 40 * 1024 * 1024
+VMEM_BYTES = 36 * 1024 * 1024
 HELD = pltpu.VMEM
 
 

time: 94.9 us -> 94.9 us (level)
  no operation moved by 1% of the time
where the time goes in v2:
time: 94.9 us; the launch traced here: 94.6 us
  Pallas kernels  51.2 us (54%)
  waiting for transfers between devices  20.5 us (22%)
  starting transfers between devices  19 us (20%)
  matrix products  1.77 us (2%)
  between operations  0.95 us (1%)
    pallas_call x3, Pallas kernels, call(): pl.pallas_call(kernel, out_shape=out_shape, in_specs=[hbm if at in distan...  39.7 us
    all_to_all x1, waiting for transfers between devices, per_device(): lax.all_to_all(parcels, AXES, split_axis=0, concat_axis=0, tiled=True)  20.5 us
    pallas_call x1, Pallas kernels, per_device(): pl.pallas_call(functools.partial(pairs_kernel, orders=orders), grid=(inne...  11.5 us
    ppermute x2, starting transfers between devices, from_sides(): high = lax.ppermute(block_low, AXES, backward)  8.95 us
    all_to_all x1, starting transfers between devices, per_device(): lax.all_to_all(parcels, AXES, split_axis=0, concat_axis=0, tiled=True)  6.1 us
    ppermute x2, starting transfers between devices, from_sides(): low = lax.ppermute(block_high, AXES, forward)  3.98 us
  transfers between devices with their start and end apart: 5, of which 1 were waited for; matrix products, arithmetic and copies ran while one was open for 3% of the time, Pallas kernels for 42%

profile of v2, /device:TPU:4, one launch (start us, length us, event | category | flops | bytes accessed | tf_op | source)
XLA Modules:
  0.0 94.6 jit_solution(16205940857433299472)
XLA Ops:
  0.6 0.0 copy-start.9
  0.6 0.0 copy-start.10
  0.7 6.1 %all-to-all-start = ((bf16[32,24,1152]{2,1,0:T(8,128)(2,1)}), bf16[32,24,1152]{2,1,0:T(8,128)(2,1)S(1)}, u32[]{:S(2)}, u32[]{:S(2)}) async-start(bf16[32,24,1152]{2,1,0:T(8,128)(2,1)} %bitcast.23), calls=%async_computation | async-start | bytes 3538944 | tf_op jit(solution)/shard_map/all_to_all | solution.py:508
  6.8 0.1 broadcast_in_dim.31
  6.9 0.1 reshape.75
  7.0 0.1 broadcast_in_dim.33
  7.1 0.1 reshape.76
  7.2 0.1 fusion.3
  7.2 0.1 reshape.81
  7.4 2.1 %collective-permute-start.2 = (f32[8,128]{1,0:T(8,128)S(1)}, f32[8,128]{1,0:T(8,128)S(1)}, u32[]{:S(2)}, u32[]{:S(2)}) collective-permute-start(f32[8,128]{1,0:T(8,128)S(1)} %get-tuple-element.28), channel_id=1, source_target_pairs={{0,1},{1,2},{2,3},{3,4},{4,5},{5,6},{6,7},{7,8},{8,9},{9,10},{10,1... | collective-permute-start | bytes 12296 | tf_op jit(solution)/shard_map/ppermute | solution.py:486
  9.5 4.4 %collective-permute-start.3 = (f32[8,128]{1,0:T(8,128)S(1)}, f32[8,128]{1,0:T(8,128)S(1)}, u32[]{:S(2)}, u32[]{:S(2)}) collective-permute-start(f32[8,128]{1,0:T(8,128)S(1)} %get-tuple-element.27), channel_id=1, source_target_pairs={{1,0},{2,1},{3,2},{4,3},{5,4},{6,5},{7,6},{8,7},{9,8},{10,9},{11,1... | collective-permute-start | bytes 12296 | tf_op jit(solution)/shard_map/ppermute | solution.py:487
  13.9 0.1 lt.29
  14.0 0.0 copy-done.4
  14.0 0.1 copy.16
  14.2 0.3 fusion.chosen_ref
  14.5 1.8 %fusion.1.gains_ref = f32[768,384]{1,0:T(8,128)} fusion(f32[89,384]{1,0:T(8,128)S(1)} %bitcast.19, s32[768]{0:T(1024)S(1)} %copy-done.6), kind=kOutput, calls=%fused_computation.3 | convolution fusion | flops 315034368 | bytes 1319424 | tf_op jit(solution)/shard_map/dot_general | solution.py:537
  16.2 11.5 %pairs.1 = (bf16[5,2,9,512,256]{4,3,2,1,0:T(8,128)(2,1)}, bf16[5,2,512,256]{3,2,1,0:T(8,128)(2,1)}, bf16[5,2,512,256]{3,2,1,0:T(8,128)(2,1)}) custom-call(f32[8,768]{1,0:T(8,128)S(1)} %concatenate.3.rows_ref), custom_call_target="tpu_custom_call" | custom-call | flops 10000000000 | bytes 41943040 | tf_op jit(solution)/shard_map/pairs/pallas_call | solution.py:542
  27.7 20.5 %all-to-all-done = bf16[32,24,1152]{2,1,0:T(8,128)(2,1)S(1)} async-done(((bf16[32,24,1152]{2,1,0:T(8,128)(2,1)}), bf16[32,24,1152]{2,1,0:T(8,128)(2,1)S(1)}, u32[]{:S(2)}, u32[]{:S(2)}) %all-to-all-start) | async-done | bytes 1769504 | tf_op jit(solution)/shard_map/all_to_all | solution.py:508
  48.2 0.7 edge_tiles.1
  48.9 1.9 %collective-permute-start = (bf16[128,1152]{1,0:T(8,128)(2,1)S(1)}, bf16[128,1152]{1,0:T(8,128)(2,1)S(1)}, u32[]{:S(2)}, u32[]{:S(2)}) collective-permute-start(bf16[128,1152]{1,0:T(8,128)(2,1)S(1)} %get-tuple-element.15.last_ref), channel_id=1, source_target_pairs={{0,1},{1,2},{2,3},{3,4},{4,5},{5,6},{6,7},{7,8},{8,9},{9,10},{10,1... | collective-permute-start | bytes 884744 | tf_op jit(solution)/shard_map/ppermute | solution.py:486
  50.8 4.5 %collective-permute-start.1 = (bf16[128,1152]{1,0:T(8,128)(2,1)S(1)}, bf16[128,1152]{1,0:T(8,128)(2,1)S(1)}, u32[]{:S(2)}, u32[]{:S(2)}) collective-permute-start(bf16[128,1152]{1,0:T(8,128)(2,1)S(1)} %get-tuple-element.16.first_ref), channel_id=1, source_target_pairs={{1,0},{2,1},{3,2},{4,3},{5,4},{6,5},{7,6},{8,7},{9,8},{10,9},{11,1... | collective-permute-start | bytes 884744 | tf_op jit(solution)/shard_map/ppermute | solution.py:487
  55.4 0.0 copy-done.1
  55.4 0.0 copy-done.2
  55.4 0.0 copy-done.3
  55.4 0.0 copy-done
  55.4 27.6 %inner.1 = (bf16[768,1152]{1,0:T(8,128)(2,1)S(1)}, bf16[5,128,128]{2,1,0:T(8,128)(2,1)S(1)}, f32[5,1,128]{2,1,0:T(1,128)S(1)}, f32[8,768]{1,0:T(8,128)S(1)}) custom-call(bf16[768,768]{1,0:T(8,128)(2,1)S(1)} %fusion.chosen_ref, bf16[768,1152]{1,0:T(8,128)(2,1)S(1)} %bitcast.17, bf16[128,1152]{1,0:T(8,128)(2,1)S(1)} %get-tuple-element.16.first_ref, ...), custom_call_target="tpu_custom_call" | custom-call | flops 16777216000 | bytes 4194304 | tf_op jit(solution)/shard_map/inner/pallas_call | solution.py:470
  83.0 0.0 collective-permute-done.2.low_rows_ref
  83.0 0.0 collective-permute-done.3.high_rows_ref
  83.0 0.0 collective-permute-done.low_ref
  83.1 0.0 collective-permute-done.1.high_ref
  83.1 0.1 broadcast_in_dim.35
  83.2 11.4 %outer.1 = (bf16[768,128]{1,0:T(8,128)(2,1)}, f32[768]{0:T(1024)}, f32[3,768]{1,0:T(4,128)}) custom-call(bf16[128,1152]{1,0:T(8,128)(2,1)S(1)} %collective-permute-done.low_ref, bf16[128,1152]{1,0:T(8,128)(2,1)S(1)} %collective-permute-done.1.high_ref, bf16[768,1152]{1,0:T(8,128)(2,1)S(1)} %get-tuple-element.20.feat_ref, ...), custom_call_target="tpu_custom_call" | custom-call | flops 6710886400 | bytes 4194304 | tf_op jit(solution)/shard_map/outer/pallas_call | solution.py:470
  (28 shorter events, 0.2 us)
Async XLA Ops:
  0.6 6.2 %copy-start.9 = (s32[12,3]{0,1:T(4,128)S(1)}, s32[12,3]{0,1:T(4,128)}, u32[]{:S(2)}) copy-start(s32[12,3]{0,1:T(4,128)} %param.16) | copy-start | bytes 436
  0.6 6.5 %copy-start.10 = (s32[12]{0:T(128)S(1)}, s32[12]{0:T(128)}, u32[]{:S(2)}) copy-start(s32[12]{0:T(128)} %param.15) | copy-start | bytes 148
  0.7 6.7 %copy-start.6 = (s32[768]{0:T(1024)S(1)}, s32[768]{0:T(1024)}, u32[]{:S(2)}) copy-start(s32[768]{0:T(1024)} %param.14) | copy-start | bytes 9220
  0.7 6.7 %copy-start.7 = (f32[768,3]{0,1:T(4,128)S(1)}, f32[768,3]{0,1:T(4,128)}, u32[]{:S(2)}) copy-start(f32[768,3]{0,1:T(4,128)} %param.13) | copy-start | bytes 27652
  0.7 13.3 %copy-start.4 = (f32[89,3,128]{2,0,1:T(8,128)S(1)}, f32[89,3,128]{2,0,1:T(8,128)}, u32[]{:S(2)}) copy-start(f32[89,3,128]{2,0,1:T(8,128)} %param.18) | copy-start | bytes 410116
  0.7 13.4 %copy-start.5 = (f32[8,7,128]{2,0,1:T(8,128)S(1)}, f32[8,7,128]{2,0,1:T(8,128)}, u32[]{:S(2)}) copy-start(f32[8,7,128]{2,0,1:T(8,128)} %param.17) | copy-start | bytes 86020
  0.7 13.5 %copy-start.8 = (s32[768]{0:T(1024)S(1)}, s32[768]{0:T(1024)}, u32[]{:S(2)}) copy-start(s32[768]{0:T(1024)} %param.12) | copy-start | bytes 9220
  0.7 47.5 %all-to-all-start = ((bf16[32,24,1152]{2,1,0:T(8,128)(2,1)}), bf16[32,24,1152]{2,1,0:T(8,128)(2,1)S(1)}, u32[]{:S(2)}, u32[]{:S(2)}) async-start(bf16[32,24,1152]{2,1,0:T(8,128)(2,1)} %bitcast.23), calls=%async_computation | async-start | bytes 3538944 | tf_op jit(solution)/shard_map/all_to_all | solution.py:508
  7.4 75.6 %collective-permute-start.2 = (f32[8,128]{1,0:T(8,128)S(1)}, f32[8,128]{1,0:T(8,128)S(1)}, u32[]{:S(2)}, u32[]{:S(2)}) collective-permute-start(f32[8,128]{1,0:T(8,128)S(1)} %get-tuple-element.28), channel_id=1, source_target_pairs={{0,1},{1,2},{2,3},{3,4},{4,5},{5,6},{6,7},{7,8},{8,9},{9,10},{10,1... | collective-permute-start | bytes 12296 | tf_op jit(solution)/shard_map/ppermute | solution.py:486
  9.5 73.6 %collective-permute-start.3 = (f32[8,128]{1,0:T(8,128)S(1)}, f32[8,128]{1,0:T(8,128)S(1)}, u32[]{:S(2)}, u32[]{:S(2)}) collective-permute-start(f32[8,128]{1,0:T(8,128)S(1)} %get-tuple-element.27), channel_id=1, source_target_pairs={{1,0},{2,1},{3,2},{4,3},{5,4},{6,5},{7,6},{8,7},{9,8},{10,9},{11,1... | collective-permute-start | bytes 12296 | tf_op jit(solution)/shard_map/ppermute | solution.py:487
  27.7 27.7 %copy-start.1 = (bf16[128,128]{1,0:T(8,128)(2,1)S(1)}, bf16[128,128]{1,0:T(8,128)(2,1)}, u32[]{:S(2)}) copy-start(bf16[128,128]{1,0:T(8,128)(2,1)} %mix_ref.3) | copy-start | bytes 98308
  27.7 27.7 %copy-start.2 = (bf16[128,128]{1,0:T(8,128)(2,1)S(1)}, bf16[128,128]{1,0:T(8,128)(2,1)}, u32[]{:S(2)}) copy-start(bf16[128,128]{1,0:T(8,128)(2,1)} %self_ref.3) | copy-start | bytes 98308
  27.7 27.7 %copy-start.3 = (f32[128]{0:T(128)S(1)}, f32[128]{0:T(128)}, u32[]{:S(2)}) copy-start(f32[128]{0:T(128)} %param.21) | copy-start | bytes 1540
  48.2 7.2 %copy-start = (f32[768,384]{1,0:T(8,128)S(1)}, f32[768,384]{1,0:T(8,128)}, u32[]{:S(2)}) copy-start(f32[768,384]{1,0:T(8,128)} %fusion.1.gains_ref) | copy-start | bytes 3538948
  48.9 34.1 %collective-permute-start = (bf16[128,1152]{1,0:T(8,128)(2,1)S(1)}, bf16[128,1152]{1,0:T(8,128)(2,1)S(1)}, u32[]{:S(2)}, u32[]{:S(2)}) collective-permute-start(bf16[128,1152]{1,0:T(8,128)(2,1)S(1)} %get-tuple-element.15.last_ref), channel_id=1, source_target_pairs={{0,1},{1,2},{2,3},{3,4},{4,5},{5,6},{6,7},{7,8},{8,9},{9,10},{10,1... | collective-permute-start | bytes 884744 | tf_op jit(solution)/shard_map/ppermute | solution.py:486
  50.8 32.2 %collective-permute-start.1 = (bf16[128,1152]{1,0:T(8,128)(2,1)S(1)}, bf16[128,1152]{1,0:T(8,128)(2,1)S(1)}, u32[]{:S(2)}, u32[]{:S(2)}) collective-permute-start(bf16[128,1152]{1,0:T(8,128)(2,1)S(1)} %get-tuple-element.16.first_ref), channel_id=1, source_target_pairs={{1,0},{2,1},{3,2},{4,3},{5,4},{6,5},{7,6},{8,7},{9,8},{10,9},{11,1... | collective-permute-start | bytes 884744 | tf_op jit(solution)/shard_map/ppermute | solution.py:487
